TPU v7x, 1024 devices: a whole 4x4x32 slice. The times are simulated.
1024 devices in a mesh: dp: 16 (over x, y), group: 64 (over z, core).
Axes of the slice: x: 4, y: 4, z: 32, core: 2. Of those that a mesh axis runs over, the one named last changes fastest.
Arguments:
- grad_parts: bfloat16 [16, 64, 640, 640], P('dp', None, 'group'), may hold values from -0.29882812 to 0.29882812
- row_extent: int32 [64], replicated, may hold values from 384 to 640, as said below
- col_extent: int32 [64], replicated, may hold values from 384 to 640, as said below
- worker: int32 [64], replicated, may hold values from 0 to 63, as said below
- fact_left: float32 [128, 640, 640], P('group', 'dp'), as said below
- fact_right: float32 [128, 640, 640], P('group', 'dp'), as said below
- root_left: bfloat16 [128, 640, 640], P('group'), as said below
- root_right: bfloat16 [128, 640, 640], P('group'), as said below
Outputs:
- new_left: float32 [128, 640, 640], P('group', 'dp')
- new_right: float32 [128, 640, 640], P('group', 'dp')
- update: bfloat16 [128, 640, 640], P('group')
Inputs may be any that keep to these rules, and one draw needn't show every extreme that they name: Each worker holds at most 2 blocks and some worker holds exactly 2; a worker that holds two blocks holds two blocks with a cut edge. `row_extent`: each entry is 384 or 640. `col_extent`: each entry is 384 or 640. `fact_left`: each slot is a symmetric matrix. `fact_right`: each slot is a symmetric matrix. `root_left`: each slot is a symmetric matrix. `root_right`: each slot is a symmetric matrix.
All inputs are finite; a program needn't handle non-finite values.
Results may differ from a plain program's by a relative error of at most 0.02.
Values may be sent and summed in bfloat16 or wider, within the bound.
A program may use at most 32 MiB of HBM per device.

v0:
```python
import jax
import jax.numpy as jnp
from jax import lax
from jax.sharding import PartitionSpec as P


def local(grad_parts, row_extent, col_extent, worker, fact_left, fact_right, root_left, root_right):
    groups = lax.axis_size("group")
    my_group = lax.axis_index("group")
    my_rank = lax.axis_index("dp")
    partial_grad = grad_parts[0]
    block_count, home_rows, block_size = partial_grad.shape
    slot_count = fact_left.shape[0]
    own_cols = fact_left.shape[1]
    summed = (
        lax.psum_scatter(partial_grad, "dp", scatter_dimension=2, tiled=True)
        .astype(jnp.float32)
        .astype(jnp.bfloat16)
    )
    block_ids = jnp.arange(block_count, dtype=jnp.int32)
    earlier = (worker[:, None] == worker[None, :]) & (block_ids[None, :] < block_ids[:, None])
    rank_within = jnp.sum(earlier.astype(jnp.int32), axis=1)
    target = rank_within * groups + worker
    place_ids = jnp.arange(slot_count * groups, dtype=jnp.int32)
    placement = (place_ids[:, None] == target[None, :]).astype(jnp.bfloat16)
    flat_rows = summed.reshape(block_count, home_rows * own_cols)
    outgoing = jnp.dot(placement, flat_rows, preferred_element_type=jnp.float32).astype(
        jnp.bfloat16
    )
    outgoing = outgoing.reshape(slot_count, groups * home_rows, own_cols)
    incoming = lax.all_to_all(outgoing, "group", split_axis=1, concat_axis=1, tiled=True)
    slot_ids = jnp.arange(slot_count, dtype=jnp.int32) * groups + my_group
    chosen = (slot_ids[:, None] == target[None, :]).astype(jnp.int32)
    row_limit = jnp.sum(chosen * row_extent[None, :], axis=1)
    col_limit = jnp.sum(chosen * col_extent[None, :], axis=1)
    row_pos = jnp.arange(block_size, dtype=jnp.int32)
    col_pos = my_rank * own_cols + jnp.arange(own_cols, dtype=jnp.int32)
    inside = (row_pos[None, :, None] < row_limit[:, None, None]) & (
        col_pos[None, None, :] < col_limit[:, None, None]
    )
    grad_share = jnp.where(inside, incoming, jnp.zeros((), jnp.bfloat16))
    whole_grad = lax.all_gather(grad_share, "dp", axis=2, tiled=True)
    own_rows = lax.dynamic_slice_in_dim(whole_grad, my_rank * own_cols, own_cols, 1)
    new_left = fact_left + jnp.einsum(
        "sik,sjk->sij", own_rows, whole_grad, preferred_element_type=jnp.float32
    )
    new_right = fact_right + jnp.einsum(
        "ski,skj->sij", grad_share, whole_grad, preferred_element_type=jnp.float32
    )
    right_cols = lax.dynamic_slice_in_dim(root_right, my_rank * own_cols, own_cols, 2)
    mixed_grad = jnp.einsum(
        "sik,skj->sij", whole_grad, right_cols, preferred_element_type=jnp.float32
    ).astype(jnp.bfloat16)
    update_part = jnp.einsum(
        "sik,skj->sij", root_left, mixed_grad, preferred_element_type=jnp.float32
    )
    update_part = jnp.where(inside, update_part, jnp.zeros((), jnp.float32)).astype(jnp.bfloat16)
    update = lax.all_gather(update_part, "dp", axis=2, tiled=True)
    return (new_left, new_right, update)


def solution(mesh):
    placed = (
        P("dp", None, "group", None),
        P(),
        P(),
        P(),
        P("group", "dp", None),
        P("group", "dp", None),
        P("group", None, None),
        P("group", None, None),
    )
    return jax.shard_map(
        local,
        mesh=mesh,
        in_specs=placed,
        out_specs=(P("group", "dp", None), P("group", "dp", None), P("group", None, None)),
        check_vma=False,
    )
```

profile of v0, /device:TPU:1, one launch (start us, length us, event | category | flops | bytes accessed | tf_op | source)
XLA Modules:
  0.0 390.0 jit_solution(16881432876653136824)
XLA Ops:
  7.2 0.7 all-reduce.3.cloned.1.call-update
  7.9 1.3 dynamic-slice
  9.9 0.9 convert_reduce_fusion
  10.8 0.7 multiply_add_fusion
  11.4 164.5 %all-reduce.3.cloned.1.call-done = bf16[64,10,640]{2,0,1:T(8,128)(2,1)} async-done(((bf16[64,10,640]{2,0,1:T(8,128)(2,1)}), bf16[64,10,640]{2,0,1:T(8,128)(2,1)}) %all-reduce.3.cloned.1.call-update) | async-done | bytes 819216
  176.0 1.1 constant_dynamic-slice_fusion
  177.0 0.1 copy.25
  177.2 0.2 convolution_convert_fusion.1
  177.4 0.1 copy.26
  177.5 0.4 reshape.81
  177.9 0.3 copy.37
  178.3 1.0 reshape.85
  179.2 25.2 %all-to-all-start = ((bf16[64,2,400]{2,1,0:T(2,128)(2,1)}), bf16[64,2,400]{2,1,0:T(2,128)(2,1)S(1)}, u32[]{:S(2)}, u32[]{:S(2)}) async-start(bf16[64,2,400]{2,1,0:T(2,128)(2,1)} %reshape.85), calls=%async_computation | async-start | bytes 262144 | tf_op jit(solution)/shard_map/all_to_all | solution.py:31
  204.6 0.2 fusion.7
  204.9 30.2 %all-to-all-done = bf16[64,2,400]{2,1,0:T(2,128)(2,1)S(1)} async-done(((bf16[64,2,400]{2,1,0:T(2,128)(2,1)}), bf16[64,2,400]{2,1,0:T(2,128)(2,1)S(1)}, u32[]{:S(2)}, u32[]{:S(2)}) %all-to-all-start) | async-done | bytes 102432 | tf_op jit(solution)/shard_map/all_to_all | solution.py:31
  235.1 0.4 reshape.86
  235.6 0.2 copy.28
  235.7 0.7 and_select_fusion
  236.6 58.9 %all-gather.3.cloned.1.call-done = bf16[2,640,640]{1,2,0:T(8,128)(2,1)} async-done(((bf16[2,640,40]{1,2,0:T(8,128)(2,1)}), bf16[2,640,640]{1,2,0:T(8,128)(2,1)}) %all-gather.3.cloned.1.call-update) | async-done | bytes 1638416 | tf_op jit(solution)/shard_map/all_gather | solution.py:42
  295.4 3.5 fusion.1
  298.9 2.3 convolution_add_fusion.1
  301.2 1.4 convolution_add_fusion
  302.6 77.4 %all-gather.5.cloned.1.call-done = bf16[2,640,640]{1,2,0:T(8,128)(2,1)} async-done(((bf16[2,640,40]{1,2,0:T(8,128)(2,1)}), bf16[2,640,640]{1,2,0:T(8,128)(2,1)}) %all-gather.5.cloned.1.call-update) | async-done | bytes 1638416 | tf_op jit(solution)/shard_map/all_gather | solution.py:58
  380.0 3.5 copy.31
  (21 shorter events, 0.3 us)
Async XLA Ops:
  7.2 288.3 %copy-start = (bf16[2,640,640]{2,1,0:T(8,128)(2,1)S(1)}, bf16[2,640,640]{2,1,0:T(8,128)(2,1)}, u32[]{:S(2)}) copy-start(bf16[2,640,640]{2,1,0:T(8,128)(2,1)} %param.14) | copy-start | bytes 4915204
  7.2 168.8 %all-reduce.3.cloned.1.call-start = ((), (), s32[]{:S(2)}) async-start(), calls=%async_computation.3 | async-start | bytes 1638400
  7.9 196.6 %copy-start.4 = (s32[64]{0:T(128)S(1)}, s32[64]{0:T(128)}, u32[]{:S(2)}) copy-start(s32[64]{0:T(128)} %param.9) | copy-start | bytes 772
  7.9 196.6 %copy-start.5 = (s32[64]{0:T(128)S(1)}, s32[64]{0:T(128)}, u32[]{:S(2)}) copy-start(s32[64]{0:T(128)} %param.10) | copy-start | bytes 772
  179.2 55.9 %all-to-all-start = ((bf16[64,2,400]{2,1,0:T(2,128)(2,1)}), bf16[64,2,400]{2,1,0:T(2,128)(2,1)S(1)}, u32[]{:S(2)}, u32[]{:S(2)}) async-start(bf16[64,2,400]{2,1,0:T(2,128)(2,1)} %reshape.85), calls=%async_computation | async-start | bytes 262144 | tf_op jit(solution)/shard_map/all_to_all | solution.py:31
  204.5 91.0 %all-gather.3.cloned.1.call-start = ((), (), s32[]{:S(2)}) async-start(), calls=%async_computation.1 | async-start | bytes 1740800 | tf_op jit(solution)/shard_map/all_gather | solution.py:42
  236.5 143.5 %all-gather.5.cloned.1.call-start = ((), (), s32[]{:S(2)}) async-start(), calls=%async_computation.2 | async-start | bytes 1740800 | tf_op jit(solution)/shard_map/all_gather | solution.py:58
  295.4 3.5 copy-start.1
  298.9 2.3 copy-start.2
  298.9 2.3 copy-start.3
Sparse Core Ops, SparseCore 0:
  11.3 164.5 all-reduce.2
  236.6 58.7 all-gather.2
  300.2 79.6 all-gather.4
where the time goes:
time: 390 us
  waiting for transfers between devices  332 us (85%)
  starting transfers between devices  25.3 us (6%)
  between operations  14.5 us (4%)
  local copies, waits for them, and re-layouts  8.46 us (2%)
  matrix products  7.29 us (2%)
    unnamed x4, waiting for transfers between devices  165 us
    all_gather x1, waiting for transfers between devices, local(): update = lax.all_gather(update_part, 'dp', axis=2, tiled=True)  77.4 us
    all_gather x1, waiting for transfers between devices, local(): whole_grad = lax.all_gather(grad_share, 'dp', axis=2, tiled=True)  58.9 us
    all_to_all x1, waiting for transfers between devices, local(): lax.all_to_all(outgoing, 'group', split_axis=1, concat_axis=1, tiled=True)  30.2 us
    all_to_all x1, starting transfers between devices, local(): lax.all_to_all(outgoing, 'group', split_axis=1, concat_axis=1, tiled=True)  25.2 us
  transfers between devices with their start and end apart: 4, of which 4 were waited for; matrix products, arithmetic and copies ran while one was open for 2% of the time, Pallas kernels for 0%

commit v1 on v0

v1 whole, which is shorter than its diff:
```python
import functools

import jax
import jax.numpy as jnp
from jax import lax
from jax.experimental import pallas as pl
from jax.experimental.pallas import tpu as pltpu
from jax.sharding import PartitionSpec as P

MESH = pl.DeviceIdType.MESH
LANES = 128
PAIR = 2
ROW_GROUPS = 3
RING = 4
VMEM_BYTES = 60 * 1024 * 1024


def exchange_kernel(
    sizes,
    worker_hbm,
    grad_ref,
    full_ref,
    worker_ref,
    recv_ref,
    slot_ref,
    chosen_ref,
    worker_sem,
    rs_send,
    rs_recv,
    z_send,
    z_recv,
    ag_send,
    ag_recv,
):
    ranks, groups, blocks, pairs, tiles = sizes
    pieces = tiles * ROW_GROUPS
    slots = full_ref.shape[1]
    my_rank = lax.axis_index("dp")
    my_group = lax.axis_index("group")
    pltpu.make_async_copy(worker_hbm, worker_ref, worker_sem).start()
    barrier = pltpu.get_barrier_semaphore()

    def greet_rank(step, carry):
        pl.semaphore_signal(
            barrier,
            inc=1,
            device_id=(lax.rem(my_rank + step, ranks), my_group),
            device_id_type=MESH,
        )
        return carry

    def greet_group(step, carry):
        pl.semaphore_signal(
            barrier,
            inc=1,
            device_id=(my_rank, lax.rem(my_group + step, groups)),
            device_id_type=MESH,
        )
        return carry

    lax.fori_loop(1, ranks, greet_rank, 0)
    lax.fori_loop(1, groups, greet_group, 0)

    pl.semaphore_wait(barrier, ranks + groups - 2)

    def piece_rows(rank, half):
        first = PAIR * (2 * lax.rem(rank, ROW_GROUPS) + half)
        lanes = pl.multiple_of((rank // ROW_GROUPS) * LANES, LANES)
        return grad_ref.at[pl.ds(first, PAIR), :, pl.ds(lanes, LANES)]

    def when_held(rank, half, act):
        held = rank < pieces
        if half:
            held = held & (lax.rem(rank, ROW_GROUPS) < ROW_GROUPS - 1)

        @pl.when(held)
        def _():
            act()

    def scatter_each(half, act):
        def step_to(step, carry):
            target = lax.rem(my_rank + step, ranks)

            def go():
                act(
                    pltpu.make_async_remote_copy(
                        src_ref=piece_rows(target, half),
                        dst_ref=recv_ref.at[half, my_rank],
                        send_sem=rs_send.at[half, target],
                        recv_sem=rs_recv.at[half, my_rank],
                        device_id=(target, my_group),
                        device_id_type=MESH,
                    )
                )

            when_held(target, half, go)
            return carry

        lax.fori_loop(1, ranks, step_to, 0)

    halves = range(2)
    for half in halves:
        scatter_each(half, lambda copy: copy.start())
        own = pltpu.make_async_copy(
            piece_rows(my_rank, half), recv_ref.at[half, my_rank], rs_recv.at[half, my_rank]
        )
        when_held(my_rank, half, own.start)

    depth = PAIR * blocks
    place_rows = PAIR * slots * groups

    def lay_out_places():
        lane = lax.broadcasted_iota(jnp.int32, (8, depth), 1)
        block_of = lax.rem(lane, blocks)

        def lay_out(block, held_by):
            return jnp.where(block_of == block, worker_ref[block], held_by)

        held_by = lax.fori_loop(0, blocks, lay_out, jnp.zeros_like(lane), unroll=8)

        def count_earlier(block, order):
            same = (held_by == worker_ref[block]) & (block_of > block)
            return order + same.astype(jnp.int32)

        order = lax.fori_loop(0, blocks, count_earlier, jnp.zeros_like(lane), unroll=8)
        place = PAIR * (slots * held_by + order) + lane // blocks
        row = lax.broadcasted_iota(jnp.int32, (place_rows, depth), 0)
        chosen_ref[...] = jnp.where(row == place[0:1], 1.0, 0.0).astype(jnp.bfloat16)

    pltpu.make_async_copy(worker_hbm, worker_ref, worker_sem).wait()
    when_held(my_rank, 0, lay_out_places)

    def spread_copy(half, target):
        return pltpu.make_async_remote_copy(
            src_ref=slot_ref.at[half, target],
            dst_ref=landing(half),
            send_sem=z_send.at[half],
            recv_sem=z_recv.at[half],
            device_id=(my_rank, target),
            device_id_type=MESH,
        )

    def pair_of(rank, half):
        return 2 * lax.rem(rank, ROW_GROUPS) + half

    def landing(half):
        return full_ref.at[
            my_rank // ROW_GROUPS, :, my_group, pair_of(my_rank, half)
        ]

    def spread(half):
        total = jnp.zeros((PAIR, blocks, LANES), jnp.float32)
        for step in range(ranks):
            source = lax.rem(my_rank + (ranks - step), ranks)
            arrived = recv_ref.at[half, source]
            pltpu.make_async_copy(arrived, arrived, rs_recv.at[half, source]).wait()
            total = total + recv_ref[half, source].astype(jnp.float32)
        total = total.reshape(depth, LANES).astype(jnp.bfloat16)
        placed = jnp.dot(chosen_ref[...], total, preferred_element_type=jnp.float32)
        slot_ref.at[half].reshape(place_rows, LANES)[...] = placed.astype(jnp.bfloat16)

        def spread_start(hop, carry):
            reach = groups // 2 - (hop + 1) // 2
            target = lax.rem(
                my_group + jnp.where(lax.rem(hop, 2) == 0, reach, groups - reach), groups
            )
            spread_copy(half, target).start()
            return carry

        lax.fori_loop(0, groups - 1, spread_start, 0)
        pltpu.make_async_copy(
            slot_ref.at[half, my_group], landing(half), z_recv.at[half]
        ).start()

    def spread_wait(half):
        mine = full_ref.at[my_rank // ROW_GROUPS, :, :, pair_of(my_rank, half)]
        pltpu.make_async_copy(mine, mine, z_recv.at[half]).wait()

    def spread_finish(half):
        sent = slot_ref.at[half, pl.ds(0, groups - 1)]
        pltpu.make_async_copy(sent, sent, z_send.at[half]).wait()

    for half in halves:
        when_held(my_rank, half, functools.partial(spread, half))

    side = RING
    my_x, my_y = my_rank // side, lax.rem(my_rank, side)
    chunks = [(slot, half) for half in halves for slot in range(slots)]

    def rank_at(slot, first, second):
        first, second = lax.rem(first, side), lax.rem(second, side)
        return side * first + second if slot == 0 else side * second + first

    def relay_copy(slot, half, source, target, index):
        piece = full_ref.at[
            source // ROW_GROUPS, slot, :, pair_of(source, half)
        ]
        return pltpu.make_async_remote_copy(
            src_ref=piece,
            dst_ref=piece,
            send_sem=ag_send.at[slot, half, index],
            recv_sem=ag_recv.at[slot, half, source],
            device_id=(target, my_group),
            device_id_type=MESH,
        )

    def relays(slot, half):
        first, second = (my_x, my_y) if slot == 0 else (my_y, my_x)
        at = functools.partial(rank_at, slot)
        ahead = (slot + half) % 2 == 0
        onward = (side - 1, 1) if ahead else (1, side - 1)
        lines = (0, 1, side - 1, side // 2)
        moves = {"own": [], "near": [], "far": [], "cross": [], "last": []}
        me = at(first, second)
        moves["own"] = [
            (me, at(first + 1, second)),
            (me, at(first + side - 1, second)),
            (me, at(first, second + 1)),
            (me, at(first, second + side - 1)),
        ]
        for line in (1, side - 1):
            source = at(first + line, second)
            targets = [at(first, second + 1), at(first, second + side - 1)]
            if line == onward[0]:
                targets = [at(first + onward[1], second)] + targets
            moves["near"].append((source, targets))
        source = at(first + side // 2, second)
        moves["far"].append((source, [at(first, second + 1), at(first, second + side - 1)]))
        for line in lines:
            for turn in (1, side - 1):
                source = at(first + line, second + turn)
                targets = [at(first, second + onward[1])] if turn == onward[0] else []
                moves["cross"].append((source, targets))
            moves["last"].append((at(first + line, second + side // 2), []))
        return moves

    plans = {chunk: relays(*chunk) for chunk in chunks}
    started = {chunk: [] for chunk in chunks}

    def relay_start(slot, half, source, targets):
        sends = []
        for target in targets:
            index = len(started[slot, half])
            started[slot, half].append((source, target))
            sends.append(relay_copy(slot, half, source, target, index))
        when_held(source, half, lambda: [copy.start() for copy in sends])

    def relay_own(half):
        for slot in range(slots):
            moves = plans[slot, half]["own"]
            relay_start(slot, half, moves[0][0], [target for _, target in moves])

    def relay_on(stage, half):
        for slot in range(slots):
            for source, targets in plans[slot, half][stage]:
                arrival = relay_copy(slot, half, source, my_rank, 0)
                when_held(source, half, arrival.wait_recv)
                if targets:
                    relay_start(slot, half, source, targets)

    when_held(my_rank, 0, lambda: spread_wait(0))
    relay_own(0)
    relay_on("near", 0)
    when_held(my_rank, 1, lambda: spread_wait(1))
    relay_own(1)
    for stage, half in (
        ("far", 0),
        ("near", 1),
        ("cross", 0),
        ("far", 1),
        ("cross", 1),
        ("last", 0),
        ("last", 1),
    ):
        relay_on(stage, half)

    for half in halves:
        scatter_each(half, lambda copy: copy.wait_send())
        when_held(my_rank, half, functools.partial(spread_finish, half))
    for slot, half in chunks:
        for index, (source, target) in enumerate(started[slot, half]):
            sent = relay_copy(slot, half, source, target, index)
            when_held(source, half, sent.wait_send)


def exchange(grad, worker, sizes):
    ranks, groups, blocks, pairs, tiles = sizes
    slots = 2
    return pl.pallas_call(
        functools.partial(exchange_kernel, sizes),
        out_shape=jax.ShapeDtypeStruct(
            (tiles, slots, groups, pairs, PAIR, LANES), jnp.bfloat16
        ),
        in_specs=[
            pl.BlockSpec(memory_space=pl.ANY),
            pl.BlockSpec(memory_space=pl.ANY),
        ],
        out_specs=pl.BlockSpec(memory_space=pltpu.VMEM),
        scratch_shapes=[
            pltpu.SMEM((blocks,), jnp.int32),
            pltpu.VMEM((2, ranks, PAIR, blocks, LANES), jnp.bfloat16),
            pltpu.VMEM((2, groups, slots, PAIR, LANES), jnp.bfloat16),
            pltpu.VMEM((PAIR * slots * groups, PAIR * blocks), jnp.bfloat16),
            pltpu.SemaphoreType.DMA,
            pltpu.SemaphoreType.DMA((2, ranks)),
            pltpu.SemaphoreType.DMA((2, ranks)),
            pltpu.SemaphoreType.DMA((2,)),
            pltpu.SemaphoreType.DMA((2,)),
            pltpu.SemaphoreType.DMA((slots, 2, ranks)),
            pltpu.SemaphoreType.DMA((slots, 2, ranks)),
        ],
        compiler_params=pltpu.CompilerParams(
            collective_id=0, has_side_effects=True, vmem_limit_bytes=VMEM_BYTES
        ),
    )(worker, grad)


def update_kernel(
    worker_ref,
    row_extent_ref,
    col_extent_ref,
    full_ref,
    fact_left_ref,
    fact_right_ref,
    root_left_ref,
    root_right_ref,
    new_left_ref,
    new_right_ref,
    update_ref,
    grad_ref,
):
    slot = pl.program_id(0)
    my_rank = lax.axis_index("dp")
    my_group = lax.axis_index("group")
    blocks = worker_ref.shape[0]
    tiles, _, groups, pairs, _, _ = full_ref.shape
    size = root_left_ref.shape[1]
    own = fact_left_ref.shape[1]

    def find(block, carry):
        seen, rows, cols = carry
        mine = worker_ref[block] == my_group
        hit = mine & (seen == slot)
        rows = jnp.where(hit, row_extent_ref[block], rows)
        cols = jnp.where(hit, col_extent_ref[block], cols)
        return seen + mine.astype(jnp.int32), rows, cols

    zero = jnp.int32(0)
    _, row_limit, col_limit = lax.fori_loop(0, blocks, find, (zero, zero, zero), unroll=True)

    row = lax.broadcasted_iota(jnp.int32, (size, LANES), 0)
    lane = lax.broadcasted_iota(jnp.int32, (size, LANES), 1)
    for tile in range(tiles):
        part = full_ref.at[tile, 0].reshape(size, LANES)[...]
        inside = (row < row_limit) & (tile * LANES + lane < col_limit)
        grad_ref[:, tile * LANES : (tile + 1) * LANES] = jnp.where(
            inside, part.astype(jnp.float32), 0.0
        ).astype(jnp.bfloat16)
    grad = grad_ref[...]

    mixed = jnp.dot(grad, root_right_ref[0], preferred_element_type=jnp.float32)
    product = jnp.dot(
        root_left_ref[0], mixed.astype(jnp.bfloat16), preferred_element_type=jnp.float32
    )
    out_row = lax.broadcasted_iota(jnp.int32, (size, size), 0)
    out_col = lax.broadcasted_iota(jnp.int32, (size, size), 1)
    inside = (out_row < row_limit) & (out_col < col_limit)
    update_ref[0] = jnp.where(inside, product, 0.0).astype(jnp.bfloat16)

    start = my_rank * own
    pick = lax.broadcasted_iota(jnp.int32, (size, LANES), 0) == start + lane
    pick = jnp.where(pick & (lane < own), 1.0, 0.0).astype(jnp.bfloat16)
    own_cols = jnp.dot(grad, pick, preferred_element_type=jnp.float32).astype(jnp.bfloat16)
    own_rows = lax.dot_general(
        pick, grad, (((0,), (0,)), ((), ())), preferred_element_type=jnp.float32
    ).astype(jnp.bfloat16)
    left = lax.dot_general(
        own_rows, grad, (((1,), (1,)), ((), ())), preferred_element_type=jnp.float32
    )
    right = lax.dot_general(
        own_cols, grad, (((0,), (0,)), ((), ())), preferred_element_type=jnp.float32
    )
    new_left_ref[0] = fact_left_ref[0] + left[:own]
    new_right_ref[0] = fact_right_ref[0] + right[:own]


def precondition(full, worker, row_extent, col_extent, fact_left, fact_right, root_left, root_right):
    slots, own, size = fact_left.shape
    tiles, _, groups, pairs, _, _ = full.shape
    smem = pl.BlockSpec(memory_space=pltpu.SMEM)
    fact = pl.BlockSpec((1, own, size), lambda slot: (slot, 0, 0))
    root = pl.BlockSpec((1, size, size), lambda slot: (slot, 0, 0))
    return pl.pallas_call(
        update_kernel,
        grid=(slots,),
        out_shape=(
            jax.ShapeDtypeStruct(fact_left.shape, jnp.float32),
            jax.ShapeDtypeStruct(fact_right.shape, jnp.float32),
            jax.ShapeDtypeStruct(root_left.shape, jnp.bfloat16),
        ),
        in_specs=[
            smem,
            smem,
            smem,
            pl.BlockSpec(
                (tiles, 1, groups, pairs, PAIR, LANES), lambda slot: (0, slot, 0, 0, 0, 0)
            ),
            fact,
            fact,
            root,
            root,
        ],
        out_specs=(fact, fact, root),
        scratch_shapes=[pltpu.VMEM((size, size), jnp.bfloat16)],
        compiler_params=pltpu.CompilerParams(vmem_limit_bytes=VMEM_BYTES),
    )(worker, row_extent, col_extent, full, fact_left, fact_right, root_left, root_right)


def solution(mesh):
    placed = (
        P("dp", None, "group", None),
        P(),
        P(),
        P(),
        P("group", "dp", None),
        P("group", "dp", None),
        P("group", None, None),
        P("group", None, None),
    )

    def local(grad_parts, row_extent, col_extent, worker, fact_left, fact_right, root_left, root_right):
        grad = jnp.transpose(grad_parts[0], (1, 0, 2))
        rows, blocks, size = grad.shape
        sizes = (
            mesh.shape["dp"],
            mesh.shape["group"],
            blocks,
            rows // PAIR,
            size // LANES,
        )
        full = exchange(grad, worker, sizes)
        return precondition(
            full, worker, row_extent, col_extent, fact_left, fact_right, root_left, root_right
        )

    return jax.shard_map(
        local,
        mesh=mesh,
        in_specs=placed,
        out_specs=(P("group", "dp", None), P("group", "dp", None), P("group", None, None)),
        check_vma=False,
    )
```

time: 390 us -> 86.8 us (0.22)
  waiting for transfers between devices: 332 us -> 0 us
  Pallas kernels: 0 us -> 84.7 us
  starting transfers between devices: 25.3 us -> 0 us
  between operations: 14.5 us -> 0.64 us
  local copies, waits for them, and re-layouts: 8.46 us -> 0 us
  matrix products: 7.29 us -> 0 us
    unnamed x4 -> x0, waiting for transfers between devices: 165 us -> none
    all_gather x2 -> x0, waiting for transfers between devices: 136 us -> none  [the longest x1 77.4 us: local(): update = lax.all_gather(update_part, 'dp', axis=2, tiled=True)]
    pallas_call x0 -> x2, Pallas kernels: none -> 84.7 us  [the longest x1 76.3 us: exchange(): pl.pallas_call(functools.partial(exchange_kernel, sizes), out_shape=jax.S...]
    all_to_all x1 -> x0, waiting for transfers between devices: 30.2 us -> none  [local(): lax.all_to_all(outgoing, 'group', split_axis=1, concat_axis=1, tiled=True)]
    all_to_all x1 -> x0, starting transfers between devices: 25.2 us -> none  [local(): lax.all_to_all(outgoing, 'group', split_axis=1, concat_axis=1, tiled=True)]
    unnamed x17 -> x0, local copies, waits for them, and re-layouts: 7.32 us -> none
    dot_general x4 -> x0, matrix products: 7.29 us -> none  [the longest x1 3.45 us: local(): jnp.einsum('sik,skj->sij', root_left, mixed_grad, preferred_element_type=...]
  transfers between devices with their start and end apart: 4 -> 0, of which waited for: 4 -> 0; matrix products, arithmetic and copies ran while one was open for 2% -> 0% of each run, Pallas kernels for 0% -> 0%
where the time goes in v1:
time: 86.8 us; the launch traced here: 85.3 us
  Pallas kernels  84.7 us (98%)
    pallas_call x1, Pallas kernels, exchange(): pl.pallas_call(functools.partial(exchange_kernel, sizes), out_shape=jax.S...  76.3 us
    pallas_call x1, Pallas kernels, precondition(): pl.pallas_call(update_kernel, grid=(slots,), out_shape=(jax.ShapeDtypeStr...  8.35 us

profile of v1, /device:TPU:1, one launch (start us, length us, event | category | flops | bytes accessed | tf_op | source)
XLA Modules:
  0.0 85.3 jit_solution(13805467792145268927)
XLA Ops:
  0.6 76.3 %shard_map.103.full_ref = bf16[5,2,64,5,2,128]{5,4,3,2,1,0:T(2,128)(2,1)} custom-call(s32[64]{0:T(128)} %worker_ref.1, bf16[10,64,640]{2,1,0:T(8,128)(2,1)} %bitcast.3), custom_call_target="tpu_custom_call" | custom-call | tf_op jit(solution)/shard_map/pallas_call | solution.py:289
  77.0 8.3 %shard_map.104 = (f32[2,40,640]{2,1,0:T(8,128)}, f32[2,40,640]{2,1,0:T(8,128)}, bf16[2,640,640]{2,1,0:T(8,128)(2,1)}) custom-call(s32[64]{0:T(128)} %worker_ref.1, s32[64]{0:T(128)} %row_extent_ref.1, s32[64]{0:T(128)} %col_extent_ref.1, bf16[5,2,64,5,2,128]{5,4,3,2,1,0:T(2,128)(2,1)} %shard_map.103.full_ref, f32[2,40,640]{2,1,0:T(8,128)} %fact_left_ref.1, ...), custom_call_target="tpu_custom_call" | custom-call | tf_op jit(solution)/shard_map/pallas_call | solution.py:393

commit v2 on v1

--- a/solution.py
+++ b/solution.py
@@ -12,7 +12,13 @@
 PAIR = 2
 ROW_GROUPS = 3
 RING = 4
+SQUARE = 8
 VMEM_BYTES = 60 * 1024 * 1024
+
+
+def split_rank(rank):
+    tile = lax.div(rank * 11, 32)
+    return tile, rank - ROW_GROUPS * tile
 
 
 def exchange_kernel(
@@ -25,6 +31,7 @@
     slot_ref,
     chosen_ref,
     worker_sem,
+    ready_sem,
     rs_send,
     rs_recv,
     z_send,
@@ -49,29 +56,41 @@
         )
         return carry
 
-    def greet_group(step, carry):
+    row_first = SQUARE * lax.div(my_group, SQUARE)
+    place = lax.rem(my_group, SQUARE)
+
+    def in_row(step):
+        return row_first + lax.rem(place + step, SQUARE)
+
+    def in_column(step):
+        return lax.rem(my_group + SQUARE * step, groups)
+
+    def signal(semaphore, member):
         pl.semaphore_signal(
-            barrier,
-            inc=1,
-            device_id=(my_rank, lax.rem(my_group + step, groups)),
-            device_id_type=MESH,
-        )
+            semaphore, inc=1, device_id=(my_rank, member), device_id_type=MESH
+        )
+
+    def greet_row(step, carry):
+        signal(barrier, in_row(step))
         return carry
 
+    rows = groups // SQUARE
     lax.fori_loop(1, ranks, greet_rank, 0)
-    lax.fori_loop(1, groups, greet_group, 0)
-
-    pl.semaphore_wait(barrier, ranks + groups - 2)
+    lax.fori_loop(1, SQUARE, greet_row, 0)
+    signal(barrier, in_column(1))
+    signal(barrier, in_column(rows - 1))
+    pl.semaphore_wait(barrier, ranks + SQUARE)
 
     def piece_rows(rank, half):
-        first = PAIR * (2 * lax.rem(rank, ROW_GROUPS) + half)
-        lanes = pl.multiple_of((rank // ROW_GROUPS) * LANES, LANES)
+        tile, row_group = split_rank(rank)
+        first = PAIR * (2 * row_group + half)
+        lanes = pl.multiple_of(tile * LANES, LANES)
         return grad_ref.at[pl.ds(first, PAIR), :, pl.ds(lanes, LANES)]
 
     def when_held(rank, half, act):
         held = rank < pieces
         if half:
-            held = held & (lax.rem(rank, ROW_GROUPS) < ROW_GROUPS - 1)
+            held = held & (split_rank(rank)[1] < ROW_GROUPS - 1)
 
         @pl.when(held)
         def _():
@@ -99,12 +118,14 @@
         lax.fori_loop(1, ranks, step_to, 0)
 
     halves = range(2)
-    for half in halves:
+    def scatter_start(half):
         scatter_each(half, lambda copy: copy.start())
         own = pltpu.make_async_copy(
             piece_rows(my_rank, half), recv_ref.at[half, my_rank], rs_recv.at[half, my_rank]
         )
         when_held(my_rank, half, own.start)
+
+    scatter_start(0)
 
     depth = PAIR * blocks
     place_rows = PAIR * slots * groups
@@ -127,8 +148,23 @@
         row = lax.broadcasted_iota(jnp.int32, (place_rows, depth), 0)
         chosen_ref[...] = jnp.where(row == place[0:1], 1.0, 0.0).astype(jnp.bfloat16)
 
+    rounds = rows // 2
+
+    def tell(index):
+        signal(ready_sem.at[index], in_column(1))
+        signal(ready_sem.at[index], in_column(rows - 1))
+
+    def hear(index):
+        pl.semaphore_wait(ready_sem.at[index], 2)
+
+    tell(0)
     pltpu.make_async_copy(worker_hbm, worker_ref, worker_sem).wait()
     when_held(my_rank, 0, lay_out_places)
+    for index in range(1, rounds):
+        hear(index - 1)
+        tell(index)
+    scatter_each(0, lambda copy: copy.wait_send())
+    scatter_start(1)
 
     def spread_copy(half, target):
         return pltpu.make_async_remote_copy(
@@ -140,13 +176,9 @@
             device_id_type=MESH,
         )
 
-    def pair_of(rank, half):
-        return 2 * lax.rem(rank, ROW_GROUPS) + half
-
     def landing(half):
-        return full_ref.at[
-            my_rank // ROW_GROUPS, :, my_group, pair_of(my_rank, half)
-        ]
+        tile, row_group = split_rank(my_rank)
+        return full_ref.at[tile, :, my_group, 2 * row_group + half]
 
     def spread(half):
         total = jnp.zeros((PAIR, blocks, LANES), jnp.float32)
@@ -173,13 +205,15 @@
         ).start()
 
     def spread_wait(half):
-        mine = full_ref.at[my_rank // ROW_GROUPS, :, :, pair_of(my_rank, half)]
+        tile, row_group = split_rank(my_rank)
+        mine = full_ref.at[tile, :, :, 2 * row_group + half]
         pltpu.make_async_copy(mine, mine, z_recv.at[half]).wait()
 
     def spread_finish(half):
         sent = slot_ref.at[half, pl.ds(0, groups - 1)]
         pltpu.make_async_copy(sent, sent, z_send.at[half]).wait()
 
+    hear(rounds - 1)
     for half in halves:
         when_held(my_rank, half, functools.partial(spread, half))
 
@@ -192,9 +226,8 @@
         return side * first + second if slot == 0 else side * second + first
 
     def relay_copy(slot, half, source, target, index):
-        piece = full_ref.at[
-            source // ROW_GROUPS, slot, :, pair_of(source, half)
-        ]
+        tile, row_group = split_rank(source)
+        piece = full_ref.at[tile, slot, :, 2 * row_group + half]
         return pltpu.make_async_remote_copy(
             src_ref=piece,
             dst_ref=piece,
@@ -258,10 +291,10 @@
                 if targets:
                     relay_start(slot, half, source, targets)
 
-    when_held(my_rank, 0, lambda: spread_wait(0))
+    when_held(my_rank, 0, functools.partial(spread_wait, 0))
     relay_own(0)
     relay_on("near", 0)
-    when_held(my_rank, 1, lambda: spread_wait(1))
+    when_held(my_rank, 1, functools.partial(spread_wait, 1))
     relay_own(1)
     for stage, half in (
         ("far", 0),
@@ -274,8 +307,8 @@
     ):
         relay_on(stage, half)
 
+    scatter_each(1, lambda copy: copy.wait_send())
     for half in halves:
-        scatter_each(half, lambda copy: copy.wait_send())
         when_held(my_rank, half, functools.partial(spread_finish, half))
     for slot, half in chunks:
         for index, (source, target) in enumerate(started[slot, half]):
@@ -302,6 +335,7 @@
             pltpu.VMEM((2, groups, slots, PAIR, LANES), jnp.bfloat16),
             pltpu.VMEM((PAIR * slots * groups, PAIR * blocks), jnp.bfloat16),
             pltpu.SemaphoreType.DMA,
+            pltpu.SemaphoreType.REGULAR((groups // SQUARE // 2,)),
             pltpu.SemaphoreType.DMA((2, ranks)),
             pltpu.SemaphoreType.DMA((2, ranks)),
             pltpu.SemaphoreType.DMA((2,)),

time: 86.8 us -> 78.2 us (0.901)
  the two profiles are of different devices: /device:TPU:1 before, /device:TPU:6 now
where the time goes in v2:
time: 78.2 us; the launch traced here: 78 us
  Pallas kernels  77.4 us (99%)
    pallas_call x1, Pallas kernels, exchange(): pl.pallas_call(functools.partial(exchange_kernel, sizes), out_shape=jax.S...  69 us
    pallas_call x1, Pallas kernels, precondition(): pl.pallas_call(update_kernel, grid=(slots,), out_shape=(jax.ShapeDtypeStr...  8.34 us

profile of v2, /device:TPU:6, one launch (start us, length us, event | category | flops | bytes accessed | tf_op | source)
XLA Modules:
  0.0 78.0 jit_solution(13647820894014404493)
XLA Ops:
  0.6 69.0 %shard_map.103.full_ref = bf16[5,2,64,5,2,128]{5,4,3,2,1,0:T(2,128)(2,1)} custom-call(s32[64]{0:T(128)} %worker_ref.1, bf16[10,64,640]{2,1,0:T(8,128)(2,1)} %bitcast.3), custom_call_target="tpu_custom_call" | custom-call | tf_op jit(solution)/shard_map/pallas_call | solution.py:322
  69.7 8.3 %shard_map.104 = (f32[2,40,640]{2,1,0:T(8,128)}, f32[2,40,640]{2,1,0:T(8,128)}, bf16[2,640,640]{2,1,0:T(8,128)(2,1)}) custom-call(s32[64]{0:T(128)} %worker_ref.1, s32[64]{0:T(128)} %row_extent_ref.1, s32[64]{0:T(128)} %col_extent_ref.1, bf16[5,2,64,5,2,128]{5,4,3,2,1,0:T(2,128)(2,1)} %shard_map.103.full_ref, f32[2,40,640]{2,1,0:T(8,128)} %fact_left_ref.1, ...), custom_call_target="tpu_custom_call" | custom-call | tf_op jit(solution)/shard_map/pallas_call | solution.py:427

commit v3 on v2

--- a/solution.py
+++ b/solution.py
@@ -243,7 +243,7 @@
         ahead = (slot + half) % 2 == 0
         onward = (side - 1, 1) if ahead else (1, side - 1)
         lines = (0, 1, side - 1, side // 2)
-        moves = {"own": [], "near": [], "far": [], "cross": [], "last": []}
+        moves = {"own": [], "first": [], "second": [], "third": [], "last": []}
         me = at(first, second)
         moves["own"] = [
             (me, at(first + 1, second)),
@@ -256,14 +256,15 @@
             targets = [at(first, second + 1), at(first, second + side - 1)]
             if line == onward[0]:
                 targets = [at(first + onward[1], second)] + targets
-            moves["near"].append((source, targets))
+            moves["first"].append((source, targets))
         source = at(first + side // 2, second)
-        moves["far"].append((source, [at(first, second + 1), at(first, second + side - 1)]))
-        for line in lines:
+        moves["second"].append((source, [at(first, second + 1), at(first, second + side - 1)]))
+        stages = ("first", "second", "second", "third")
+        for line, stage in zip(lines, stages):
             for turn in (1, side - 1):
                 source = at(first + line, second + turn)
                 targets = [at(first, second + onward[1])] if turn == onward[0] else []
-                moves["cross"].append((source, targets))
+                moves[stage].append((source, targets))
             moves["last"].append((at(first + line, second + side // 2), []))
         return moves
 
@@ -293,15 +294,15 @@
 
     when_held(my_rank, 0, functools.partial(spread_wait, 0))
     relay_own(0)
-    relay_on("near", 0)
+    relay_on("first", 0)
     when_held(my_rank, 1, functools.partial(spread_wait, 1))
     relay_own(1)
     for stage, half in (
-        ("far", 0),
-        ("near", 1),
-        ("cross", 0),
-        ("far", 1),
-        ("cross", 1),
+        ("second", 0),
+        ("first", 1),
+        ("third", 0),
+        ("second", 1),
+        ("third", 1),
         ("last", 0),
         ("last", 1),
     ):

time: 78.2 us -> 78.9 us (level)
  the two profiles are of different devices: /device:TPU:6 before, /device:TPU:1 now
where the time goes in v3:
time: 78.9 us; the launch traced here: 77.7 us
  Pallas kernels  77 us (98%)
    pallas_call x1, Pallas kernels, exchange(): pl.pallas_call(functools.partial(exchange_kernel, sizes), out_shape=jax.S...  68.7 us
    pallas_call x1, Pallas kernels, precondition(): pl.pallas_call(update_kernel, grid=(slots,), out_shape=(jax.ShapeDtypeStr...  8.34 us

profile of v3, /device:TPU:1, one launch (start us, length us, event | category | flops | bytes accessed | tf_op | source)
XLA Modules:
  0.0 77.7 jit_solution(12712573280898995322)
XLA Ops:
  0.6 68.7 %shard_map.103.full_ref = bf16[5,2,64,5,2,128]{5,4,3,2,1,0:T(2,128)(2,1)} custom-call(s32[64]{0:T(128)} %worker_ref.1, bf16[10,64,640]{2,1,0:T(8,128)(2,1)} %bitcast.3), custom_call_target="tpu_custom_call" | custom-call | tf_op jit(solution)/shard_map/pallas_call | solution.py:323
  69.3 8.3 %shard_map.104 = (f32[2,40,640]{2,1,0:T(8,128)}, f32[2,40,640]{2,1,0:T(8,128)}, bf16[2,640,640]{2,1,0:T(8,128)(2,1)}) custom-call(s32[64]{0:T(128)} %worker_ref.1, s32[64]{0:T(128)} %row_extent_ref.1, s32[64]{0:T(128)} %col_extent_ref.1, bf16[5,2,64,5,2,128]{5,4,3,2,1,0:T(2,128)(2,1)} %shard_map.103.full_ref, f32[2,40,640]{2,1,0:T(8,128)} %fact_left_ref.1, ...), custom_call_target="tpu_custom_call" | custom-call | tf_op jit(solution)/shard_map/pallas_call | solution.py:428
